TPU v7x, 32 devices: a whole 2x2x4 slice. The times are simulated.
32 devices in a mesh: sec: 2 (over core), grp: 4 (over z), col: 4 (over y, x).
Axes of the slice: x: 2, y: 2, z: 4, core: 2. Of those that a mesh axis runs over, the one named last changes fastest.
Arguments:
- fields: float32 [2, 64, 128, 512], P('sec', 'col', 'grp'), may hold values from -4 to 4
- soil_type: int32 [64, 128, 512], P(None, 'grp', 'col'), may hold values from 0 to 7
- surface: float32 [128, 512], P('grp', 'col'), may hold values from -8 to 8
- heat_cond: float32 [8], replicated, may hold values from 0.5 to 3
- heat_capacity: float32 [8], replicated, may hold values from 1 to 3
- porosity: float32 [8], replicated, may hold values from 0.3 to 0.55
- sat_cond: float32 [8], replicated, may hold values from 0.2 to 2
- vg_alpha: float32 [8], replicated, may hold values from 0.5 to 3
Outputs:
- advanced: float32 [2, 64, 128, 512], P('sec', 'col', 'grp')
All inputs are finite; a program needn't handle non-finite values.
Results may differ from a plain program's by a relative error of at most 0.0003.
Values sent between devices are 32-bit elements; how exact they have to be, the bound alone decides.
A program may use at most 128 MiB of HBM per device.

v0:
```python
import functools
import jax
import jax.numpy as jnp
from jax import lax
from jax.experimental import pallas as pl
from jax.experimental.pallas import tpu as pltpu
from jax.sharding import PartitionSpec as P

OUTER = 2
INNER = 3
CHUNK = 4
ROWS = 40
COLS = 256
MESH = pl.DeviceIdType.MESH

heat_side = 0.2
heat_vert = 8.0
storage = 0.001
flow_side = 0.002
flow_vert = 1.5
elevation = 0.1


def harmonic(a, b):
    return 2.0 * a * b / (a + b)


def sigmoid2(x):
    return 1.0 / (1.0 + jnp.exp(-2.0 * x))


def kernel(
    n_grp, n_col, fields, soil, surface, tab, out,
    own_m, oth_m, own_r, own_rc, oth_rc, own_cs, own_c, oth_c,
    soil_r, soil_rc, soil_cs, soil_c,
    res, it_r, it_rc, it_cs, it_c, res2,
    xw, vb, bI, sI, aI, rI, kb,
    loc_sem, a2a_s, a2a_r, sec_s, sec_r, row_s, row_r, col_s, col_r, fin_s, fin_r,
):
    sec = lax.axis_index("sec")
    g = lax.axis_index("grp")
    c = lax.axis_index("col")
    nz, nx, ny = soil.shape
    zs = fields.shape[1]
    is_heat = sec == 0
    up_ok, down_ok = g > 0, g < n_grp - 1
    left_ok, right_ok = c > 0, c < n_col - 1

    barrier = pltpu.get_barrier_semaphore()
    for k in range(1, n_col):
        pl.semaphore_signal(barrier, inc=1, device_id={"col": lax.rem(c + k, n_col)}, device_id_type=MESH)
    pl.semaphore_signal(barrier, inc=1, device_id={"sec": 1 - sec}, device_id_type=MESH)

    @pl.when(up_ok)
    def _():
        pl.semaphore_signal(barrier, inc=1, device_id={"grp": g - 1}, device_id_type=MESH)

    @pl.when(down_ok)
    def _():
        pl.semaphore_signal(barrier, inc=1, device_id={"grp": g + 1}, device_id_type=MESH)

    beside = jnp.where(up_ok, 1, 0) + jnp.where(down_ok, 1, 0)
    pl.semaphore_wait(barrier, n_col + beside)

    def remote(src, dst, s, r, **where):
        return pltpu.make_async_remote_copy(
            src_ref=src, dst_ref=dst, send_sem=s, recv_sem=r, device_id=where, device_id_type=MESH
        )

    def two_way(axis, index, count, sends, dst, ssem, rsem, low_ok, high_ok):
        ahead = remote(sends[0], dst.at[0], ssem.at[0], rsem.at[0], **{axis: lax.rem(index + 1, count)})
        back = remote(sends[1], dst.at[1], ssem.at[1], rsem.at[1], **{axis: lax.rem(index + count - 1, count)})

        def start():
            @pl.when(high_ok)
            def _():
                ahead.start()

            @pl.when(low_ok)
            def _():
                back.start()

        def wait():
            @pl.when(high_ok)
            def _():
                ahead.wait_send()
                back.wait_recv()

            @pl.when(low_ok)
            def _():
                back.wait_send()
                ahead.wait_recv()

            @pl.when(jnp.logical_not(low_ok))
            def _():
                dst[0] = jnp.zeros(dst.shape[1:], dst.dtype)

            @pl.when(jnp.logical_not(high_ok))
            def _():
                dst[1] = jnp.zeros(dst.shape[1:], dst.dtype)

        return start, wait

    def rows_of(src, dst, slot):
        sends = (src.at[:, pl.ds(nx - 8, 8), :], src.at[:, pl.ds(0, 8), :])
        return two_way("grp", g, n_grp, sends, dst, row_s.at[slot], row_r.at[slot], up_ok, down_ok)

    def cols_of(src, dst, slot):
        return two_way(
            "col", c, n_col, (src.at[0], src.at[1]), dst, col_s.at[slot], col_r.at[slot], left_ok, right_ok
        )

    lane = lax.broadcasted_iota(jnp.int32, (ROWS, ny), 1)
    sub8 = lax.broadcasted_iota(jnp.int32, (8, ny), 0)

    def levels(body, carry, down=True):
        def chunk(i, carry):
            for u in range(CHUNK):
                step = i * CHUNK + u
                carry = body(step if down else nz - 1 - step, carry)
            return carry

        return lax.fori_loop(0, nz // CHUNK, chunk, carry)

    def pack(m, r2, rc, cs):
        def body(z, carry):
            ahead, back = carry
            tile = jnp.where(sub8 < 4, r2[1, z], r2[0, z])
            rc[z] = tile
            plane = jnp.concatenate([m[z], tile], axis=0)
            mine = lax.shift_right_logical(lane, 1) == z
            ahead = jnp.where(mine, pltpu.roll(plane, lax.rem(2 * z + 2, ny), 1), ahead)
            back = jnp.where(mine, pltpu.roll(plane, 2 * z, 1), back)
            return (ahead, back)

        zero = jnp.zeros((ROWS, ny), m.dtype)
        ahead, back = levels(body, (zero, zero))
        cs[0] = ahead
        cs[1] = back

    def wide(m, rc, cc, z):
        tile = jnp.concatenate([m[z], rc[z]], axis=0)
        right = pltpu.roll(cc[1], lax.rem(ny - 2 * z, ny), 1)
        left = pltpu.roll(cc[0], ny - 2 - 2 * z, 1)
        return jnp.concatenate([tile, jnp.where(lane < 64, right, left)], axis=1)

    soil_start, soil_wait = rows_of(soil, soil_r, 0)
    local = pltpu.make_async_copy(
        fields.at[0, :, :, pl.ds(pl.multiple_of(c * ny, ny), ny)], own_m.at[pl.ds(c * zs, zs)], loc_sem.at[0]
    )
    moves = []
    for k in range(1, n_col):
        to = lax.rem(c + k, n_col)
        moves.append(
            remote(
                fields.at[0, :, :, pl.ds(pl.multiple_of(to * ny, ny), ny)],
                own_m.at[pl.ds(c * zs, zs)],
                a2a_s.at[k - 1], a2a_r.at[k - 1], col=to,
            )
        )
    for move in moves:
        move.start()
    local.start()
    soil_start()
    soil_wait()
    pack(soil, soil_r, soil_rc, soil_cs)
    soilc_start, soilc_wait = cols_of(soil_cs, soil_c, 0)
    soilc_start()
    local.wait()
    for move in moves:
        move.wait()

    other = 1 - sec
    swap_m = remote(own_m, oth_m, sec_s.at[0], sec_r.at[0], sec=other)
    swap_r = remote(own_rc, oth_rc, sec_s.at[1], sec_r.at[1], sec=other)
    swap_c = remote(own_c, oth_c, sec_s.at[2], sec_r.at[2], sec=other)
    row_start, row_wait = rows_of(own_m, own_r, 1)
    row_start()
    swap_m.start()
    row_wait()
    pack(own_m, own_r, own_rc, own_cs)
    col_start, col_wait = cols_of(own_cs, own_c, 1)
    col_start()
    swap_r.start()
    col_wait()
    swap_c.start()
    soilc_wait()
    swap_m.wait()
    swap_r.wait()
    swap_c.wait()

    own = (own_m, own_rc, own_c)
    oth = (oth_m, oth_rc, oth_c)

    def looker(kind):
        b0, b1, b2 = (kind & 1) != 0, (kind & 2) != 0, (kind & 4) != 0

        def look(row):
            t = [tab[row, i] for i in range(8)]
            q = [jnp.where(b0, t[2 * i + 1], t[2 * i]) for i in range(4)]
            return jnp.where(b2, jnp.where(b1, q[3], q[2]), jnp.where(b1, q[1], q[0]))

        return look

    def state(temper, head, look):
        liquid = sigmoid2(temper)
        alpha, poro = look(4), look(2)
        suction = jnp.maximum(-head, 0.0)
        a_s = alpha * suction
        satur = lax.rsqrt(1.0 + a_s * a_s)
        return liquid, alpha, poro, suction, satur

    one = jnp.ones((ROWS, COLS), jnp.float32)
    row_i = lax.broadcasted_iota(jnp.int32, (ROWS, COLS), 0)
    col_i = lax.broadcasted_iota(jnp.int32, (ROWS, COLS), 1)
    free = ((row_i <= nx) | (row_i == ROWS - 1)) & ((col_i <= ny) | (col_i == COLS - 1))

    def heat_setup():
        kb[0] = one
        kb[nz + 1] = one

        def first(z, carry):
            temper, head, kind = wide(*own, z), wide(*oth, z), wide(soil, soil_rc, soil_c, z)
            look = looker(kind)
            liquid, alpha, poro, suction, satur = state(temper, head, look)
            moist = poro * (0.1 + 0.9 * satur)
            kb[z + 1] = look(0) * (1.0 + moist * (1.0 - liquid))
            xw[z] = temper
            cap = looker(soil[z])(1)
            lm = 4.0 * moist[:nx, :ny]
            bI[z, :nx, :ny] = cap
            bI[z, :nx, ny:] = lm
            sI[z, :nx, :ny] = cap * temper[:nx, :ny] + lm * liquid[:nx, :ny]
            return carry

        levels(first, 0)

        def second(z, carry):
            kap = kb[z + 1]
            mid = kap[:nx, :ny]
            sI[z, :nx, ny:] = heat_side * harmonic(mid, pltpu.roll(kap, ROWS - 1, 0)[:nx, :ny])
            aI[z, :nx, :ny] = heat_side * harmonic(mid, pltpu.roll(kap, 1, 0)[:nx, :ny])
            aI[z, :nx, ny:] = heat_side * harmonic(mid, pltpu.roll(kap, COLS - 1, 1)[:nx, :ny])
            rI[z, :nx, :ny] = heat_side * harmonic(mid, pltpu.roll(kap, 1, 1)[:nx, :ny])
            has = jnp.where(z < nz - 1, heat_vert, 0.0)
            rI[z, :nx, ny:] = has * harmonic(mid, kb[z + 2, :nx, :ny])
            return carry

        levels(second, 0)
        sI[0, :nx, :ny] = sI[0, :nx, :ny] + 2.0 * heat_vert * kb[1, :nx, :ny] * surface[...]

    def heat_solve(dst):
        def forward(z, carry):
            above, ratio, value = carry
            x = xw[z]
            t = x[:nx, :ny]
            cap, lm = bI[z, :nx, :ny], bI[z, :nx, ny:]
            f = sigmoid2(t)
            apparent = cap + lm * f * (1.0 - f) * 2.0
            lateral = sI[z, :nx, ny:] * (pltpu.roll(x, ROWS - 1, 0)[:nx, :ny] - t)
            lateral += aI[z, :nx, :ny] * (pltpu.roll(x, 1, 0)[:nx, :ny] - t)
            lateral += aI[z, :nx, ny:] * (pltpu.roll(x, COLS - 1, 1)[:nx, :ny] - t)
            lateral += rI[z, :nx, :ny] * (pltpu.roll(x, 1, 1)[:nx, :ny] - t)
            right = apparent * t - (cap * t + lm * f) + sI[z, :nx, :ny] + lateral
            below = rI[z, :nx, ny:]
            inv = 1.0 / (apparent + above + below + above * ratio)
            ratio = -below * inv
            value = (right + above * value) * inv
            vb[z, :nx, :ny] = value
            vb[z, :nx, ny:] = ratio
            return (below, ratio, value)

        zero = jnp.zeros((nx, ny), jnp.float32)
        levels(forward, (2.0 * heat_vert * kb[1, :nx, :ny], zero, zero))

        def backward(z, lower):
            solved = vb[z, :nx, :ny] - vb[z, :nx, ny:] * lower
            dst[z] = solved
            return solved

        levels(backward, zero, down=False)

    def flow_setup():
        kb[0] = one
        kb[nz + 1] = one

        def first(z, carry):
            temper, head, kind = wide(*oth, z), wide(*own, z), wide(soil, soil_rc, soil_c, z)
            look = looker(kind)
            liquid, alpha, poro, suction, satur = state(temper, head, look)
            cube = satur * satur * satur
            kb[z + 1] = look(3) * cube * jnp.exp(-2.0 * (1.0 - liquid))
            vb[z] = storage + poro * 0.9 * alpha * alpha * suction * cube
            xw[z] = head
            return carry

        levels(first, 0)

        def second(z, carry):
            above, ratio = carry
            hyd, cap, x = kb[z + 1], vb[z], xw[z]
            has = jnp.where(z < nz - 1, flow_vert * 0.5, 0.0)
            drain = jnp.where(z < nz - 1, 0.0, elevation)
            below = has * (hyd + kb[z + 2])
            side = flow_side * hyd
            inv = 1.0 / (cap + above + below + 4.0 * side - above * ratio)
            ratio = below * inv
            base = cap * x + elevation * (above - below) - drain * hyd
            bI[z] = jnp.where(free, base * inv, x)
            sI[z] = jnp.where(free, side * inv, 0.0)
            aI[z] = jnp.where(free, above * inv, 0.0)
            rI[z] = jnp.where(free, ratio, 0.0)
            return (below, ratio)

        zero = jnp.zeros((ROWS, COLS), jnp.float32)
        levels(second, (zero, zero))

    def flow_solve(dst):
        for inner in range(INNER):
            last = inner == INNER - 1
            h, w = (nx, ny) if last else (ROWS, COLS)

            def forward(z, value):
                x = xw[z]
                near = pltpu.roll(x, 1, 0) + pltpu.roll(x, ROWS - 1, 0)
                near = near[:h, :w] + (pltpu.roll(x, 1, 1) + pltpu.roll(x, COLS - 1, 1))[:h, :w]
                value = bI[z, :h, :w] + sI[z, :h, :w] * near + aI[z, :h, :w] * value
                vb[z, :h, :w] = value
                return value

            zero = jnp.zeros((h, w), jnp.float32)
            levels(forward, zero)

            def backward(z, lower):
                solved = vb[z, :h, :w] + rI[z, :h, :w] * lower
                if last:
                    dst[z] = solved
                else:
                    xw[z] = solved
                return solved

            levels(backward, zero, down=False)

    @pl.when(is_heat)
    def _():
        heat_setup()
        heat_solve(res)

    @pl.when(jnp.logical_not(is_heat))
    def _():
        flow_setup()
        flow_solve(res)

    itr_start, itr_wait = rows_of(res, it_r, 2)
    itr_start()
    itr_wait()
    pack(res, it_r, it_rc, it_cs)
    itc_start, itc_wait = cols_of(it_cs, it_c, 2)
    itc_start()
    itc_wait()

    @pl.when(is_heat)
    def _():
        def fill(z, carry):
            xw[z] = wide(res, it_rc, it_c, z)
            return carry

        levels(fill, 0)
        heat_solve(res2)

    @pl.when(jnp.logical_not(is_heat))
    def _():
        def fill(z, carry):
            x = wide(res, it_rc, it_c, z)
            xw[z] = x
            bI[z] = jnp.where(free, bI[z], x)
            return carry

        levels(fill, 0)
        flow_solve(res2)

    lanes = pl.ds(pl.multiple_of(c * ny, ny), ny)
    moves = []
    for k in range(1, n_col):
        to = lax.rem(c + k, n_col)
        moves.append(
            remote(res2.at[pl.ds(to * zs, zs)], out.at[0, :, :, lanes], fin_s.at[k - 1], fin_r.at[k - 1], col=to)
        )
    local = pltpu.make_async_copy(res2.at[pl.ds(c * zs, zs)], out.at[0, :, :, lanes], loc_sem.at[1])
    for move in moves:
        move.start()
    local.start()
    local.wait()
    for move in moves:
        move.wait()


def solution(mesh):
    n_grp, n_col = mesh.shape["grp"], mesh.shape["col"]

    def on_device(fields, soil_type, surface, heat_cond, heat_capacity, porosity, sat_cond, vg_alpha):
        tab = jnp.stack([heat_cond, heat_capacity, porosity, sat_cond, vg_alpha])
        nz, nx, ny = soil_type.shape
        f32, i32 = jnp.float32, jnp.int32
        whole = lambda t: pltpu.VMEM((nz, nx, ny), t)
        tile = lambda t: pltpu.VMEM((nz, 8, ny), t)
        pair = lambda t: pltpu.VMEM((2, nz, 8, ny), t)
        strip = lambda t: pltpu.VMEM((2, ROWS, ny), t)
        field = pltpu.VMEM((nz, ROWS, COLS), f32)
        dma = lambda *s: pltpu.SemaphoreType.DMA(s)
        scratch = [
            whole(f32), whole(f32), pair(f32), tile(f32), tile(f32), strip(f32), strip(f32), strip(f32),
            pair(i32), tile(i32), strip(i32), strip(i32),
            whole(f32), pair(f32), tile(f32), strip(f32), strip(f32), whole(f32),
            field, field, field, field, field, field, pltpu.VMEM((nz + 2, ROWS, COLS), f32),
            dma(2), dma(n_col - 1), dma(n_col - 1), dma(3), dma(3), dma(3, 2), dma(3, 2), dma(3, 2), dma(3, 2),
            dma(n_col - 1), dma(n_col - 1),
        ]
        anywhere = pl.BlockSpec(memory_space=pl.ANY)
        vmem = pl.BlockSpec(memory_space=pltpu.VMEM)
        return pl.pallas_call(
            functools.partial(kernel, n_grp, n_col),
            out_shape=jax.ShapeDtypeStruct(fields.shape, f32),
            in_specs=[anywhere, vmem, vmem, pl.BlockSpec(memory_space=pltpu.SMEM)],
            out_specs=anywhere,
            scratch_shapes=scratch,
            compiler_params=pltpu.CompilerParams(
                collective_id=0, has_side_effects=True, vmem_limit_bytes=48 * 2**20
            ),
            name="step",
        )(fields, soil_type, surface, tab)

    in_specs = (
        P("sec", "col", "grp", None), P(None, "grp", "col"), P("grp", "col"),
        P(), P(), P(), P(), P(),
    )
    return jax.shard_map(
        on_device, mesh=mesh, in_specs=in_specs, out_specs=P("sec", "col", "grp", None), check_vma=False
    )
```

profile of v0, /device:TPU:1, one launch (start us, length us, event | category | flops | bytes accessed | tf_op | source)
XLA Modules:
  0.0 79.0 jit_solution(13176662900759651417)
XLA Ops:
  0.0 0.0 copy-start.6
  0.0 0.0 copy-start.7
  0.0 0.0 copy-start.3
  0.0 0.0 copy-start.4
  0.0 0.0 copy-start.5
  0.0 0.6 copy-done.6
  0.7 0.0 copy-done.7
  0.7 0.0 copy-done.3
  0.7 0.0 copy-done.4
  0.7 0.0 copy-done.5
  0.7 0.0 copy-start
  0.7 1.2 %copy-done = f32[1,16,32,512]{3,2,1,0:T(8,128)S(1)} copy-done((f32[1,16,32,512]{3,2,1,0:T(8,128)S(1)}, f32[1,16,32,512]{3,2,1,0:T(8,128)}, u32[]{:S(2)}) %copy-start) | copy-done | bytes 1048600
  2.0 0.0 copy-start.1
  2.0 1.2 %copy-done.1 = s32[64,32,128]{2,1,0:T(8,128)S(1)} copy-done((s32[64,32,128]{2,1,0:T(8,128)S(1)}, s32[64,32,128]{2,1,0:T(8,128)}, u32[]{:S(2)}) %copy-start.1) | copy-done | bytes 1048600
  3.2 0.0 copy-start.2
  3.2 0.7 copy-done.2
  3.9 74.1 %step.1 = f32[1,16,32,512]{3,2,1,0:T(8,128)S(1)} custom-call(f32[1,16,32,512]{3,2,1,0:T(8,128)S(1)} %copy-done, s32[64,32,128]{2,1,0:T(8,128)S(1)} %copy-done.1, f32[32,128]{1,0:T(8,128)S(1)} %copy-done.2, f32[5,8]{1,0:T(8,128)S(1)} %stack.23.tab), custom_call_target="tpu_custom_call" | custom-call | tf_op jit(solution)/shard_map/step/pallas_call | solution.py:421
  78.0 1.0 %copy.10 = f32[1,16,32,512]{3,2,1,0:T(8,128)} copy(f32[1,16,32,512]{3,2,1,0:T(8,128)S(1)} %step.1) | data formatting | bytes 2097152
  (1 shorter events, 0.0 us)
Async XLA Ops:
  0.0 0.7 copy-start.6
  0.0 0.7 copy-start.7
  0.0 0.7 copy-start.3
  0.0 0.7 copy-start.4
  0.0 0.7 copy-start.5
  0.7 1.2 %copy-start = (f32[1,16,32,512]{3,2,1,0:T(8,128)S(1)}, f32[1,16,32,512]{3,2,1,0:T(8,128)}, u32[]{:S(2)}) copy-start(f32[1,16,32,512]{3,2,1,0:T(8,128)} %fields.1) | copy-start | bytes 3145732
  2.0 1.2 %copy-start.1 = (s32[64,32,128]{2,1,0:T(8,128)S(1)}, s32[64,32,128]{2,1,0:T(8,128)}, u32[]{:S(2)}) copy-start(s32[64,32,128]{2,1,0:T(8,128)} %soil.1) | copy-start | bytes 3145732
  3.2 0.7 copy-start.2
where the time goes:
time: 79.2 us; the launch traced here: 79 us
  Pallas kernels  74.1 us (94%)
  local copies, waits for them, and re-layouts  4.85 us (6%)
    pallas_call x1, Pallas kernels, on_device(): pl.pallas_call(functools.partial(kernel, n_grp, n_col), out_shape=jax.Sha...  74.1 us
    unnamed x17, local copies, waits for them, and re-layouts  4.83 us

commit v1 on v0

--- a/solution.py
+++ b/solution.py
@@ -30,12 +30,13 @@
 
 
 def kernel(
-    n_grp, n_col, fields, soil, surface, tab, out,
-    own_m, oth_m, own_r, own_rc, oth_rc, own_cs, own_c, oth_c,
-    soil_r, soil_rc, soil_cs, soil_c,
-    res, it_r, it_rc, it_cs, it_c, res2,
+    n_grp, n_col, fields, soil_in, surface_in, tab_0, tab_1, tab_2, tab_3, tab_4, out,
+    soil, surface, tab,
+    own_m, oth_m, own_rc, oth_rc, own_cs, own_c, oth_c,
+    soil_rc, soil_cs, soil_c,
+    res, it_rc, it_cs, it_c, res2,
     xw, vb, bI, sI, aI, rI, kb,
-    loc_sem, a2a_s, a2a_r, sec_s, sec_r, row_s, row_r, col_s, col_r, fin_s, fin_r,
+    loc_sem, a2a_s, a2a_r, sec_s, sec_r, edge_s, edge_r, fin_s, fin_r,
 ):
     sec = lax.axis_index("sec")
     g = lax.axis_index("grp")
@@ -43,75 +44,83 @@
     nz, nx, ny = soil.shape
     zs = fields.shape[1]
     is_heat = sec == 0
-    up_ok, down_ok = g > 0, g < n_grp - 1
-    left_ok, right_ok = c > 0, c < n_col - 1
+
+    def inside(dg, dc):
+        ok = None
+        for at, d, count in ((g, dg, n_grp), (c, dc, n_col)):
+            if d:
+                here = at < count - 1 if d > 0 else at > 0
+                ok = here if ok is None else jnp.logical_and(ok, here)
+        return ok
+
+    way = [(1, 0), (-1, 0), (0, 1), (0, -1), (1, 1), (-1, 1), (1, -1), (-1, -1)]
+
+    def at_way(dg, dc):
+        return {"grp": lax.rem(g + dg + n_grp, n_grp), "col": lax.rem(c + dc + n_col, n_col)}
 
     barrier = pltpu.get_barrier_semaphore()
+    for buffer in (own_rc, soil_rc, it_rc, own_c, soil_c, it_c):
+        buffer[...] = jnp.zeros(buffer.shape, buffer.dtype)
+    met = n_col
     for k in range(1, n_col):
         pl.semaphore_signal(barrier, inc=1, device_id={"col": lax.rem(c + k, n_col)}, device_id_type=MESH)
     pl.semaphore_signal(barrier, inc=1, device_id={"sec": 1 - sec}, device_id_type=MESH)
-
-    @pl.when(up_ok)
-    def _():
-        pl.semaphore_signal(barrier, inc=1, device_id={"grp": g - 1}, device_id_type=MESH)
-
-    @pl.when(down_ok)
-    def _():
-        pl.semaphore_signal(barrier, inc=1, device_id={"grp": g + 1}, device_id_type=MESH)
-
-    beside = jnp.where(up_ok, 1, 0) + jnp.where(down_ok, 1, 0)
-    pl.semaphore_wait(barrier, n_col + beside)
+    for dg, dc in way:
+        if dg:
+            met = met + jnp.where(inside(dg, dc), 1, 0)
+
+            @pl.when(inside(dg, dc))
+            def _():
+                pl.semaphore_signal(barrier, inc=1, device_id=at_way(dg, dc), device_id_type=MESH)
+
+    pl.semaphore_wait(barrier, met)
 
     def remote(src, dst, s, r, **where):
         return pltpu.make_async_remote_copy(
             src_ref=src, dst_ref=dst, send_sem=s, recv_sem=r, device_id=where, device_id_type=MESH
         )
 
-    def two_way(axis, index, count, sends, dst, ssem, rsem, low_ok, high_ok):
-        ahead = remote(sends[0], dst.at[0], ssem.at[0], rsem.at[0], **{axis: lax.rem(index + 1, count)})
-        back = remote(sends[1], dst.at[1], ssem.at[1], rsem.at[1], **{axis: lax.rem(index + count - 1, count)})
-
-        def start():
-            @pl.when(high_ok)
-            def _():
-                ahead.start()
-
-            @pl.when(low_ok)
-            def _():
-                back.start()
+    def edges(m, rc, cs, cc, slot):
+        low, high = pl.ds(0, 2), pl.ds(nx - 2, 2)
+        above, below = pl.ds(ROWS - 2, 2), pl.ds(nx, 2)
+        parts = [
+            (m.at[:, high, :], rc.at[:, pl.ds(6, 2), :]),
+            (m.at[:, low, :], rc.at[:, pl.ds(0, 2), :]),
+            (cs.at[0], cc.at[0, pl.ds(0, nx), :]),
+            (cs.at[1], cc.at[1, pl.ds(0, nx), :]),
+            (cs.at[0, high, :], cc.at[0, above, :]),
+            (cs.at[0, low, :], cc.at[0, below, :]),
+            (cs.at[1, high, :], cc.at[1, above, :]),
+            (cs.at[1, low, :], cc.at[1, below, :]),
+        ]
+        copies = [
+            remote(src, dst, edge_s.at[slot, i], edge_r.at[slot, i], **at_way(*way[i]))
+            for i, (src, dst) in enumerate(parts)
+        ]
+
+        def start(these):
+            for i in these:
+                @pl.when(inside(*way[i]))
+                def _():
+                    copies[i].start()
+
+        start((0, 1))
+        pack(m, cs)
+        start(range(2, 8))
 
         def wait():
-            @pl.when(high_ok)
-            def _():
-                ahead.wait_send()
-                back.wait_recv()
-
-            @pl.when(low_ok)
-            def _():
-                back.wait_send()
-                ahead.wait_recv()
-
-            @pl.when(jnp.logical_not(low_ok))
-            def _():
-                dst[0] = jnp.zeros(dst.shape[1:], dst.dtype)
-
-            @pl.when(jnp.logical_not(high_ok))
-            def _():
-                dst[1] = jnp.zeros(dst.shape[1:], dst.dtype)
-
-        return start, wait
-
-    def rows_of(src, dst, slot):
-        sends = (src.at[:, pl.ds(nx - 8, 8), :], src.at[:, pl.ds(0, 8), :])
-        return two_way("grp", g, n_grp, sends, dst, row_s.at[slot], row_r.at[slot], up_ok, down_ok)
-
-    def cols_of(src, dst, slot):
-        return two_way(
-            "col", c, n_col, (src.at[0], src.at[1]), dst, col_s.at[slot], col_r.at[slot], left_ok, right_ok
-        )
+            for i, (dg, dc) in enumerate(way):
+                @pl.when(inside(dg, dc))
+                def _():
+                    copies[i].wait_send()
+
+                @pl.when(inside(-dg, -dc))
+                def _():
+                    copies[i].wait_recv()
+
+        return wait
 
     lane = lax.broadcasted_iota(jnp.int32, (ROWS, ny), 1)
-    sub8 = lax.broadcasted_iota(jnp.int32, (8, ny), 0)
 
     def levels(body, carry, down=True):
         def chunk(i, carry):
@@ -122,18 +131,17 @@
 
         return lax.fori_loop(0, nz // CHUNK, chunk, carry)
 
-    def pack(m, r2, rc, cs):
+    def pack(m, cs):
+        pair = lax.shift_right_logical(lax.broadcasted_iota(jnp.int32, (nx, ny), 1), 1)
+
         def body(z, carry):
             ahead, back = carry
-            tile = jnp.where(sub8 < 4, r2[1, z], r2[0, z])
-            rc[z] = tile
-            plane = jnp.concatenate([m[z], tile], axis=0)
-            mine = lax.shift_right_logical(lane, 1) == z
-            ahead = jnp.where(mine, pltpu.roll(plane, lax.rem(2 * z + 2, ny), 1), ahead)
-            back = jnp.where(mine, pltpu.roll(plane, 2 * z, 1), back)
+            plane = m[z]
+            ahead = jnp.where(pair == z, pltpu.roll(plane, lax.rem(2 * z + 2, ny), 1), ahead)
+            back = jnp.where(pair == z, pltpu.roll(plane, 2 * z, 1), back)
             return (ahead, back)
 
-        zero = jnp.zeros((ROWS, ny), m.dtype)
+        zero = jnp.zeros((nx, ny), m.dtype)
         ahead, back = levels(body, (zero, zero))
         cs[0] = ahead
         cs[1] = back
@@ -144,7 +152,9 @@
         left = pltpu.roll(cc[0], ny - 2 - 2 * z, 1)
         return jnp.concatenate([tile, jnp.where(lane < 64, right, left)], axis=1)
 
-    soil_start, soil_wait = rows_of(soil, soil_r, 0)
+    tabs = (tab_0, tab_1, tab_2, tab_3, tab_4)
+    loads = [pltpu.make_async_copy(soil_in, soil, loc_sem.at[2]), pltpu.make_async_copy(surface_in, surface, loc_sem.at[3])]
+    loads += [pltpu.make_async_copy(t, tab.at[i], loc_sem.at[4 + i]) for i, t in enumerate(tabs)]
     local = pltpu.make_async_copy(
         fields.at[0, :, :, pl.ds(pl.multiple_of(c * ny, ny), ny)], own_m.at[pl.ds(c * zs, zs)], loc_sem.at[0]
     )
@@ -161,33 +171,36 @@
     for move in moves:
         move.start()
     local.start()
-    soil_start()
+    for load in loads:
+        load.start()
+    loads[0].wait()
+    soil_wait = edges(soil, soil_rc, soil_cs, soil_c, 0)
+
+    other = 1 - sec
+    swaps = []
+
+    def swap(src, dst):
+        i = len(swaps)
+        swaps.append(remote(src, dst, sec_s.at[i], sec_r.at[i], sec=other))
+        swaps[i].start()
+
+    local.wait()
+    swap(own_m.at[pl.ds(c * zs, zs)], oth_m.at[pl.ds(c * zs, zs)])
+    for k, move in enumerate(moves):
+        move.wait_recv()
+        came = lax.rem(c + n_col - 1 - k, n_col)
+        swap(own_m.at[pl.ds(came * zs, zs)], oth_m.at[pl.ds(came * zs, zs)])
+    own_wait = edges(own_m, own_rc, own_cs, own_c, 1)
+    own_wait()
+    swap(own_rc, oth_rc)
+    swap(own_c, oth_c)
+    for move in moves:
+        move.wait_send()
     soil_wait()
-    pack(soil, soil_r, soil_rc, soil_cs)
-    soilc_start, soilc_wait = cols_of(soil_cs, soil_c, 0)
-    soilc_start()
-    local.wait()
-    for move in moves:
-        move.wait()
-
-    other = 1 - sec
-    swap_m = remote(own_m, oth_m, sec_s.at[0], sec_r.at[0], sec=other)
-    swap_r = remote(own_rc, oth_rc, sec_s.at[1], sec_r.at[1], sec=other)
-    swap_c = remote(own_c, oth_c, sec_s.at[2], sec_r.at[2], sec=other)
-    row_start, row_wait = rows_of(own_m, own_r, 1)
-    row_start()
-    swap_m.start()
-    row_wait()
-    pack(own_m, own_r, own_rc, own_cs)
-    col_start, col_wait = cols_of(own_cs, own_c, 1)
-    col_start()
-    swap_r.start()
-    col_wait()
-    swap_c.start()
-    soilc_wait()
-    swap_m.wait()
-    swap_r.wait()
-    swap_c.wait()
+    for load in loads[1:]:
+        load.wait()
+    for one_swap in swaps:
+        one_swap.wait()
 
     own = (own_m, own_rc, own_c)
     oth = (oth_m, oth_rc, oth_c)
@@ -351,13 +364,8 @@
         flow_setup()
         flow_solve(res)
 
-    itr_start, itr_wait = rows_of(res, it_r, 2)
-    itr_start()
-    itr_wait()
-    pack(res, it_r, it_rc, it_cs)
-    itc_start, itc_wait = cols_of(it_cs, it_c, 2)
-    itc_start()
-    itc_wait()
+    it_wait = edges(res, it_rc, it_cs, it_c, 2)
+    it_wait()
 
     @pl.when(is_heat)
     def _():
@@ -399,36 +407,35 @@
     n_grp, n_col = mesh.shape["grp"], mesh.shape["col"]
 
     def on_device(fields, soil_type, surface, heat_cond, heat_capacity, porosity, sat_cond, vg_alpha):
-        tab = jnp.stack([heat_cond, heat_capacity, porosity, sat_cond, vg_alpha])
         nz, nx, ny = soil_type.shape
         f32, i32 = jnp.float32, jnp.int32
         whole = lambda t: pltpu.VMEM((nz, nx, ny), t)
         tile = lambda t: pltpu.VMEM((nz, 8, ny), t)
-        pair = lambda t: pltpu.VMEM((2, nz, 8, ny), t)
         strip = lambda t: pltpu.VMEM((2, ROWS, ny), t)
         field = pltpu.VMEM((nz, ROWS, COLS), f32)
         dma = lambda *s: pltpu.SemaphoreType.DMA(s)
+        part = pltpu.VMEM((2, nx, ny), f32)
         scratch = [
-            whole(f32), whole(f32), pair(f32), tile(f32), tile(f32), strip(f32), strip(f32), strip(f32),
-            pair(i32), tile(i32), strip(i32), strip(i32),
-            whole(f32), pair(f32), tile(f32), strip(f32), strip(f32), whole(f32),
+            whole(i32), pltpu.VMEM((nx, ny), f32), pltpu.SMEM((5, heat_cond.shape[0]), f32),
+            whole(f32), whole(f32), tile(f32), tile(f32), part, strip(f32), strip(f32),
+            tile(i32), pltpu.VMEM((2, nx, ny), i32), strip(i32),
+            whole(f32), tile(f32), part, strip(f32), whole(f32),
             field, field, field, field, field, field, pltpu.VMEM((nz + 2, ROWS, COLS), f32),
-            dma(2), dma(n_col - 1), dma(n_col - 1), dma(3), dma(3), dma(3, 2), dma(3, 2), dma(3, 2), dma(3, 2),
+            dma(9), dma(n_col - 1), dma(n_col - 1), dma(n_col + 2), dma(n_col + 2), dma(3, 8), dma(3, 8),
             dma(n_col - 1), dma(n_col - 1),
         ]
         anywhere = pl.BlockSpec(memory_space=pl.ANY)
-        vmem = pl.BlockSpec(memory_space=pltpu.VMEM)
         return pl.pallas_call(
             functools.partial(kernel, n_grp, n_col),
             out_shape=jax.ShapeDtypeStruct(fields.shape, f32),
-            in_specs=[anywhere, vmem, vmem, pl.BlockSpec(memory_space=pltpu.SMEM)],
+            in_specs=[anywhere] * 8,
             out_specs=anywhere,
             scratch_shapes=scratch,
             compiler_params=pltpu.CompilerParams(
-                collective_id=0, has_side_effects=True, vmem_limit_bytes=48 * 2**20
+                collective_id=0, has_side_effects=True, vmem_limit_bytes=58 * 2**20
             ),
             name="step",
-        )(fields, soil_type, surface, tab)
+        )(fields, soil_type, surface, heat_cond, heat_capacity, porosity, sat_cond, vg_alpha)
 
     in_specs = (
         P("sec", "col", "grp", None), P(None, "grp", "col"), P("grp", "col"),

time: 79.2 us -> 67.1 us (0.85)
  Pallas kernels: 74.1 us -> 64.6 us
  local copies, waits for them, and re-layouts: 4.85 us -> 2.29 us
    pallas_call x1, Pallas kernels: 74.1 us -> 64.6 us  [on_device(): pl.pallas_call(functools.partial(kernel, n_grp, n_col), out_shape=jax.Sha...]
    unnamed x17 -> x1, local copies, waits for them, and re-layouts: 4.83 us -> 2.29 us
where the time goes in v1:
time: 67.1 us; the launch traced here: 66.9 us
  Pallas kernels  64.6 us (96%)
  local copies, waits for them, and re-layouts  2.29 us (3%)
    pallas_call x1, Pallas kernels, on_device(): pl.pallas_call(functools.partial(kernel, n_grp, n_col), out_shape=jax.Sha...  64.6 us
    unnamed x1, local copies, waits for them, and re-layouts  2.29 us

profile of v1, /device:TPU:1, one launch (start us, length us, event | category | flops | bytes accessed | tf_op | source)
XLA Modules:
  0.0 66.9 jit_solution(1130123805694019097)
XLA Ops:
  0.0 64.6 %step.1 = f32[1,16,32,512]{3,2,1,0:T(8,128)} custom-call(f32[1,16,32,512]{3,2,1,0:T(8,128)} %fields.1, s32[64,32,128]{2,1,0:T(8,128)} %soil_in.1, f32[32,128]{1,0:T(8,128)} %surface_in.1, f32[8]{0:T(128)} %tab_0.1, f32[8]{0:T(128)} %tab_1.1, f32[8]{0:T(128)} %tab_2.1, f32[8]{0:T(128)} %tab_3.1, f32[8]{0:T(128)} %tab_4.1), custom_call_target="tpu_custom_call" | custom-call | tf_op jit(solution)/shard_map/step/pallas_call | solution.py:428
  64.6 2.3 %copy.10 = f32[1,16,32,512]{3,2,1,0:T(8,128)} copy(f32[1,16,32,512]{3,2,1,0:T(8,128)} %step.1) | data formatting | bytes 2097152

commit v2 on v1

--- a/solution.py
+++ b/solution.py
@@ -8,7 +8,7 @@
 
 OUTER = 2
 INNER = 3
-CHUNK = 4
+CHUNK = 16
 ROWS = 40
 COLS = 256
 MESH = pl.DeviceIdType.MESH

time: 67.1 us -> 58.8 us (0.88)
  Pallas kernels: 64.6 us -> 56.4 us
    pallas_call x1, Pallas kernels: 64.6 us -> 56.4 us  [on_device(): pl.pallas_call(functools.partial(kernel, n_grp, n_col), out_shape=jax.Sha...]
where the time goes in v2:
time: 58.8 us; the launch traced here: 58.7 us
  Pallas kernels  56.4 us (96%)
  local copies, waits for them, and re-layouts  2.29 us (4%)
    pallas_call x1, Pallas kernels, on_device(): pl.pallas_call(functools.partial(kernel, n_grp, n_col), out_shape=jax.Sha...  56.4 us
    unnamed x1, local copies, waits for them, and re-layouts  2.29 us

profile of v2, /device:TPU:1, one launch (start us, length us, event | category | flops | bytes accessed | tf_op | source)
XLA Modules:
  0.0 58.7 jit_solution(2974022311401940124)
XLA Ops:
  0.0 56.4 %step.1 = f32[1,16,32,512]{3,2,1,0:T(8,128)} custom-call(f32[1,16,32,512]{3,2,1,0:T(8,128)} %fields.1, s32[64,32,128]{2,1,0:T(8,128)} %soil_in.1, f32[32,128]{1,0:T(8,128)} %surface_in.1, f32[8]{0:T(128)} %tab_0.1, f32[8]{0:T(128)} %tab_1.1, f32[8]{0:T(128)} %tab_2.1, f32[8]{0:T(128)} %tab_3.1, f32[8]{0:T(128)} %tab_4.1), custom_call_target="tpu_custom_call" | custom-call | tf_op jit(solution)/shard_map/step/pallas_call | solution.py:428
  56.4 2.3 %copy.10 = f32[1,16,32,512]{3,2,1,0:T(8,128)} copy(f32[1,16,32,512]{3,2,1,0:T(8,128)} %step.1) | data formatting | bytes 2097152

commit v3 on v2

--- a/solution.py
+++ b/solution.py
@@ -104,9 +104,7 @@
                 def _():
                     copies[i].start()
 
-        start((0, 1))
-        pack(m, cs)
-        start(range(2, 8))
+        start(range(8))
 
         def wait():
             for i, (dg, dc) in enumerate(way):
@@ -131,20 +129,26 @@
 
         return lax.fori_loop(0, nz // CHUNK, chunk, carry)
 
-    def pack(m, cs):
-        pair = lax.shift_right_logical(lax.broadcasted_iota(jnp.int32, (nx, ny), 1), 1)
-
-        def body(z, carry):
-            ahead, back = carry
-            plane = m[z]
-            ahead = jnp.where(pair == z, pltpu.roll(plane, lax.rem(2 * z + 2, ny), 1), ahead)
-            back = jnp.where(pair == z, pltpu.roll(plane, 2 * z, 1), back)
-            return (ahead, back)
-
-        zero = jnp.zeros((nx, ny), m.dtype)
-        ahead, back = levels(body, (zero, zero))
-        cs[0] = ahead
-        cs[1] = back
+    pair = lax.shift_right_logical(lax.broadcasted_iota(jnp.int32, (nx, ny), 1), 1)
+
+    def packed(z, plane, strips):
+        ahead, back = strips
+        ahead = jnp.where(pair == z, pltpu.roll(plane, lax.rem(2 * z + 2, ny), 1), ahead)
+        back = jnp.where(pair == z, pltpu.roll(plane, 2 * z, 1), back)
+        return (ahead, back)
+
+    def no_strips(dtype):
+        zero = jnp.zeros((nx, ny), dtype)
+        return (zero, zero)
+
+    def pack_slab(m, slab, strips):
+        for u in range(zs):
+            strips = packed(slab * zs + u, m[slab * zs + u], strips)
+        return strips
+
+    def keep(cs, strips):
+        cs[0] = strips[0]
+        cs[1] = strips[1]
 
     def wide(m, rc, cc, z):
         tile = jnp.concatenate([m[z], rc[z]], axis=0)
@@ -174,6 +178,7 @@
     for load in loads:
         load.start()
     loads[0].wait()
+    keep(soil_cs, levels(lambda z, strips: packed(z, soil[z], strips), no_strips(soil.dtype)))
     soil_wait = edges(soil, soil_rc, soil_cs, soil_c, 0)
 
     other = 1 - sec
@@ -186,10 +191,13 @@
 
     local.wait()
     swap(own_m.at[pl.ds(c * zs, zs)], oth_m.at[pl.ds(c * zs, zs)])
+    strips = pack_slab(own_m, c, no_strips(own_m.dtype))
     for k, move in enumerate(moves):
         move.wait_recv()
         came = lax.rem(c + n_col - 1 - k, n_col)
         swap(own_m.at[pl.ds(came * zs, zs)], oth_m.at[pl.ds(came * zs, zs)])
+        strips = pack_slab(own_m, came, strips)
+    keep(own_cs, strips)
     own_wait = edges(own_m, own_rc, own_cs, own_c, 1)
     own_wait()
     swap(own_rc, oth_rc)
@@ -262,7 +270,7 @@
         levels(second, 0)
         sI[0, :nx, :ny] = sI[0, :nx, :ny] + 2.0 * heat_vert * kb[1, :nx, :ny] * surface[...]
 
-    def heat_solve(dst):
+    def heat_solve(dst, strip=None):
         def forward(z, carry):
             above, ratio, value = carry
             x = xw[z]
@@ -286,12 +294,15 @@
         zero = jnp.zeros((nx, ny), jnp.float32)
         levels(forward, (2.0 * heat_vert * kb[1, :nx, :ny], zero, zero))
 
-        def backward(z, lower):
+        def backward(z, carry):
+            lower, strips = carry
             solved = vb[z, :nx, :ny] - vb[z, :nx, ny:] * lower
             dst[z] = solved
-            return solved
-
-        levels(backward, zero, down=False)
+            return (solved, packed(z, solved, strips) if strip is not None else strips)
+
+        unused, strips = levels(backward, (zero, no_strips(zero.dtype)), down=False)
+        if strip is not None:
+            keep(strip, strips)
 
     def flow_setup():
         kb[0] = one
@@ -328,7 +339,7 @@
         zero = jnp.zeros((ROWS, COLS), jnp.float32)
         levels(second, (zero, zero))
 
-    def flow_solve(dst):
+    def flow_solve(dst, strip=None):
         for inner in range(INNER):
             last = inner == INNER - 1
             h, w = (nx, ny) if last else (ROWS, COLS)
@@ -344,25 +355,30 @@
             zero = jnp.zeros((h, w), jnp.float32)
             levels(forward, zero)
 
-            def backward(z, lower):
+            def backward(z, carry):
+                lower, strips = carry
                 solved = vb[z, :h, :w] + rI[z, :h, :w] * lower
                 if last:
                     dst[z] = solved
+                    if strip is not None:
+                        strips = packed(z, solved, strips)
                 else:
                     xw[z] = solved
-                return solved
-
-            levels(backward, zero, down=False)
+                return (solved, strips)
+
+            unused, strips = levels(backward, (zero, no_strips(zero.dtype)), down=False)
+            if last and strip is not None:
+                keep(strip, strips)
 
     @pl.when(is_heat)
     def _():
         heat_setup()
-        heat_solve(res)
+        heat_solve(res, it_cs)
 
     @pl.when(jnp.logical_not(is_heat))
     def _():
         flow_setup()
-        flow_solve(res)
+        flow_solve(res, it_cs)
 
     it_wait = edges(res, it_rc, it_cs, it_c, 2)
     it_wait()

time: 58.8 us -> 59.3 us (level)
  no operation moved by 1% of the time
where the time goes in v3:
time: 59.3 us; the launch traced here: 59.2 us
  Pallas kernels  56.9 us (96%)
  local copies, waits for them, and re-layouts  2.29 us (4%)
    pallas_call x1, Pallas kernels, on_device(): pl.pallas_call(functools.partial(kernel, n_grp, n_col), out_shape=jax.Sha...  56.9 us
    unnamed x1, local copies, waits for them, and re-layouts  2.29 us

profile of v3, /device:TPU:1, one launch (start us, length us, event | category | flops | bytes accessed | tf_op | source)
XLA Modules:
  0.0 59.2 jit_solution(8069086475858796865)
XLA Ops:
  0.0 56.9 %step.1 = f32[1,16,32,512]{3,2,1,0:T(8,128)} custom-call(f32[1,16,32,512]{3,2,1,0:T(8,128)} %fields.1, s32[64,32,128]{2,1,0:T(8,128)} %soil_in.1, f32[32,128]{1,0:T(8,128)} %surface_in.1, f32[8]{0:T(128)} %tab_0.1, f32[8]{0:T(128)} %tab_1.1, f32[8]{0:T(128)} %tab_2.1, f32[8]{0:T(128)} %tab_3.1, f32[8]{0:T(128)} %tab_4.1), custom_call_target="tpu_custom_call" | custom-call | tf_op jit(solution)/shard_map/step/pallas_call | solution.py:444
  56.9 2.3 %copy.10 = f32[1,16,32,512]{3,2,1,0:T(8,128)} copy(f32[1,16,32,512]{3,2,1,0:T(8,128)} %step.1) | data formatting | bytes 2097152
